TPU v7x, 512 devices: a whole 4x4x16 slice. The times are simulated.
512 devices in a mesh: row: 16 (over y, x), col: 32 (over z, core).
Axes of the slice: x: 4, y: 4, z: 16, core: 2. Of those that a mesh axis runs over, the one named last changes fastest.
Arguments:
- tokens: bfloat16 [192, 12288], P('col', 'row'), may hold values from -6 to 6
- w_in: bfloat16 [12288, 49152], P('row', 'col'), may hold values from -0.0546875 to 0.0546875
- w_out: bfloat16 [49152, 12288], P('col', 'row'), may hold values from -0.02734375 to 0.02734375
- grad_out: bfloat16 [192, 12288], P('col', 'row'), may hold values from -6 to 6
Outputs:
- mixed: bfloat16 [192, 12288], P('col', 'row')
- grad_in: bfloat16 [192, 12288], P('col', 'row')
All inputs are finite; a program needn't handle non-finite values.
Results may differ from a plain program's by a relative error of at most 0.0049.
Values may be sent and summed in bfloat16 or wider, within the bound.
A program may use at most 64 MiB of HBM per device.

v0:
```python
import jax
import jax.numpy as jnp
from jax import lax
from jax.experimental import pallas as pl
from jax.experimental.pallas import tpu as pltpu
from jax.sharding import PartitionSpec as P

gelu_scale = 0.7978845608028654
cubic_coef = 0.044715

F32, BF16 = jnp.float32, jnp.bfloat16
MESH = pl.DeviceIdType.MESH
FAR = (6, -6, 2, -2)


def gelu_and_slope(values):
    squared = values * values
    bent = jnp.tanh(gelu_scale * (values + cubic_coef * squared * values))
    act = 0.5 * values * (1.0 + bent)
    slope = 0.5 * (1.0 + bent) + 0.5 * values * (1.0 - bent * bent) * gelu_scale * (
        1.0 + 3.0 * cubic_coef * squared
    )
    return act, slope


def against(left, right):
    return lax.dot_general(left, right, (((1,), (1,)), ((), ())), preferred_element_type=F32)


class Chain:
    def __init__(self, refs):
        (self.x, self.part, self.send1, self.relay, self.near1,
         self.total, self.send2, self.recv2, self.all, self.acc, self.blocks, self.sendz,
         self.nearz, self.nearz2, self.sendf, self.recvf) = refs


def chain_scratch(half, width):
    block = (48, half)
    return [
        pltpu.VMEM((96, width), BF16),
        pltpu.VMEM((4, 4) + block, F32),
        pltpu.VMEM((4, 4) + block, BF16),
        pltpu.VMEM((2, 2) + block, BF16),
        pltpu.VMEM((2, 4) + block, BF16),
        pltpu.VMEM((4,) + block, F32),
        pltpu.VMEM((4,) + block, BF16),
        pltpu.VMEM((3,) + block, BF16),
        pltpu.VMEM((4, 4) + block, BF16),
        pltpu.VMEM((128, width), F32),
        pltpu.VMEM((16, 16, half), F32),
        pltpu.VMEM((16, 16, half), BF16),
        pltpu.VMEM((2, 4, 16, half), BF16),
        pltpu.VMEM((4, 16, half), BF16),
        pltpu.VMEM((4, 16, half), BF16),
        pltpu.VMEM((4, 16, half), BF16),
    ]


CHAIN_REFS = 16
COPIES = 96


def kernel(tok_ref, win_ref, wout_ref, gout_ref, out_ref, *scratch):
    win, wout, raw, own, gathered, slope_out, slope_in = scratch[:7]
    h = Chain(scratch[7:7 + CHAIN_REFS])
    g = Chain(scratch[7 + CHAIN_REFS:7 + 2 * CHAIN_REFS])
    local_sem, send_sem, recv_sem = scratch[7 + 2 * CHAIN_REFS:]
    width = tok_ref.shape[1]
    half = width // 2

    row, col = lax.axis_index("row"), lax.axis_index("col")
    y, x = lax.div(row, 4), lax.rem(row, 4)
    z, core = lax.div(col, 2), lax.rem(col, 2)

    def at_x(step):
        return (y * 4 + lax.rem(x + step + 4, 4), col)

    def at_y(step):
        return (lax.rem(y + step + 4, 4) * 4 + x, col)

    def at_z(step):
        return (row, lax.rem(z + step + 16, 16) * 2 + core)

    other_core = (row, z * 2 + 1 - core)
    turned = (x * 4 + y, col)
    same = lax.div(3 - lax.max(x - y, y - x), 3)

    moves = [(tok_ref, raw.at[0]), (gout_ref, raw.at[1])]
    for part in range(2):
        cut = pl.ds(part * width, width)
        moves.append((win_ref.at[:, cut], win.at[2 * core + part]))
    for part in range(2):
        cut = pl.ds(part * width, width)
        moves.append((wout_ref.at[cut, :], wout.at[2 * core + part]))
    local = [pltpu.make_async_copy(src, dst, local_sem.at[n]) for n, (src, dst) in enumerate(moves)]
    for copy in local:
        copy.start()

    partners = [at_z(step) for step in (6, -6, 2, -2, 1, -1)]
    partners += [other_core, (x * 4 + y, z * 2 + core + same * (1 - 2 * core))]
    partners += [at_x(step) for step in (2, 1, -1)]
    partners += [at_y(step) for step in (2, 1, -1)]
    barrier = pltpu.get_barrier_semaphore()
    for partner in partners:
        pl.semaphore_signal(barrier, inc=1, device_id=partner, device_id_type=MESH)

    empty = jnp.zeros((2, width), F32)
    for n in range(2):
        local[n].wait()
        whole = jnp.concatenate([raw[n].astype(F32), empty], axis=0)
        folded = jnp.concatenate([whole[:, :half], whole[:, half:]], axis=0)
        own[n] = folded.astype(BF16)

    pl.semaphore_wait(barrier, len(partners))

    started = []

    def send(src, dst, device):
        n = len(started)
        copy = pltpu.make_async_remote_copy(
            src_ref=src, dst_ref=dst, send_sem=send_sem.at[n], recv_sem=recv_sem.at[n],
            device_id=device, device_id_type=MESH,
        )
        copy.start()
        started.append(copy)
        return copy

    def arrived(copies):
        for copy in copies:
            copy.wait_recv()

    slot = lax.rem(z, 4) * 4 + lax.div(z, 4)
    held = lax.rem(z + 2, 4) * 4

    def gather_far(n):
        return [send(own.at[n], gathered.at[n, slot], at_z(step)) for step in FAR]

    def gather_near(n):
        out = []
        for step, first, count in ((2, 0, 2), (-2, 2, 2), (1, 0, 4), (-1, 0, 4)):
            piece = gathered.at[n, pl.ds(held + first, count)]
            out.append(send(piece, piece, at_z(step)))
        return out

    far_in = [gather_far(0), gather_far(1)]
    pushed = []
    for part in range(2):
        src = win_ref.at[:, pl.ds(part * width, width)]
        pushed.append(send(src, win.at[2 * core + part], other_core))
    for part in range(2):
        src = wout_ref.at[pl.ds(part * width, width)]
        pushed.append(send(src, wout.at[2 * core + part], other_core))
    near_in = []
    for n in range(2):
        arrived(far_in[n])
        near_in.append(gather_near(n))

    def squeeze(c, n):
        blocks = gathered[n].astype(F32)
        left = blocks[:, :8, :].reshape(128, half)
        right = blocks[:, 8:, :].reshape(128, half)
        spread = jnp.concatenate([left, right], axis=1).astype(BF16)
        at = lax.broadcasted_iota(jnp.int32, (96, 128), 0)
        come = lax.broadcasted_iota(jnp.int32, (96, 128), 1)
        within = come & 7
        pick = jnp.where((within < 6) & (at == 6 * (come >> 3) + within), 1.0, 0.0).astype(BF16)
        c.x[...] = jnp.dot(pick, spread, preferred_element_type=F32).astype(BF16)

    def expander():
        at = lax.broadcasted_iota(jnp.int32, (128, 96), 0)
        come = lax.broadcasted_iota(jnp.int32, (128, 96), 1)
        within = at & 7
        return jnp.where((within < 6) & (come == 6 * (at >> 3) + within), 1.0, 0.0).astype(BF16)

    def quarters(value):
        return [
            value[48 * up:48 * up + 48, half * side:half * side + half]
            for up in range(2) for side in range(2)
        ]

    def relays(c, got, ahead):
        for v in range(4):
            c.send1[2, v] = got[v].astype(BF16)
        return [
            send(c.send1.at[2, pl.ds(0, 2)], c.relay.at[0], ahead(1)),
            send(c.send1.at[2, pl.ds(2, 2)], c.relay.at[1], ahead(-1)),
        ]

    def direct_up(c, got, ahead):
        for v in (2, 3):
            c.send1[1, v] = got[v].astype(BF16)
        out = [send(c.send1.at[1, pl.ds(2, 2)], c.near1.at[0, pl.ds(2, 2)], ahead(1))]
        for v in (0, 1):
            c.part[1, v] = got[v]
        return out

    def direct_down(c, got, ahead):
        for v in (0, 1):
            c.send1[3, v] = got[v].astype(BF16)
        out = [send(c.send1.at[3, pl.ds(0, 2)], c.near1.at[1, pl.ds(0, 2)], ahead(-1))]
        for v in (2, 3):
            c.part[3, v] = got[v]
        return out

    def stay(c, got):
        for v in range(4):
            c.part[0, v] = got[v]

    def passed_on(c, got, ahead):
        arrived(got[:1])
        c.send1[1, 0:2] = (c.part[1, 0:2] + c.relay[0].astype(F32)).astype(BF16)
        out = [send(c.send1.at[1, pl.ds(0, 2)], c.near1.at[0, pl.ds(0, 2)], ahead(1))]
        arrived(got[1:])
        c.send1[3, 2:4] = (c.part[3, 2:4] + c.relay[1].astype(F32)).astype(BF16)
        out.append(send(c.send1.at[3, pl.ds(2, 2)], c.near1.at[1, pl.ds(2, 2)], ahead(-1)))
        return out

    def second_sum(c, got, ahead, place):
        arrived(got)
        c.total[...] = c.part[0] + c.near1[0].astype(F32) + c.near1[1].astype(F32)
        c.send2[...] = c.total[...].astype(BF16)
        out = []
        for n, step in enumerate((2, 1, -1)):
            there = lax.rem(place + step + 4, 4)
            out.append(send(c.send2.at[there], c.recv2.at[n], ahead(step)))
        return out

    def summed(c, got, place):
        arrived(got)
        return (
            c.total[place] + c.recv2[0].astype(F32) + c.recv2[1].astype(F32) + c.recv2[2].astype(F32)
        )

    arrived(near_in[0])
    squeeze(h, 0)
    for copy in local[2:4]:
        copy.wait()
    arrived(pushed[:2])

    def hidden_part(rel):
        return quarters(jnp.dot(h.x[...], win[lax.rem(x + rel, 4)], preferred_element_type=F32))

    def grad_part(rel):
        return quarters(against(g.x[...], wout[lax.rem(y + rel, 4)]))

    relay_h = relays(h, hidden_part(2), at_x)
    direct_h = direct_up(h, hidden_part(1), at_x)
    direct_h += direct_down(h, hidden_part(3), at_x)
    stay(h, hidden_part(0))

    arrived(near_in[1])
    squeeze(g, 1)
    for copy in local[4:]:
        copy.wait()
    arrived(pushed[2:])

    relay_g = relays(g, grad_part(2), at_y)
    direct_h += passed_on(h, relay_h, at_x)
    direct_g = direct_up(g, grad_part(1), at_y)
    direct_g += direct_down(g, grad_part(3), at_y)
    stay(g, grad_part(0))
    second_h = second_sum(h, direct_h, at_y, y)
    direct_g += passed_on(g, relay_g, at_y)
    hidden = summed(h, second_h, y)
    act, slope = gelu_and_slope(hidden)
    h.all[x, y] = act.astype(BF16)

    def spread_first(c, chunk, place, ahead):
        piece = c.all.at[chunk, place]
        return [send(piece, piece, ahead(step)) for step in (2, 1, -1)]

    def spread_second(c, got, chunk, ahead):
        arrived(got)
        low, high = c.all.at[chunk, pl.ds(0, 2)], c.all.at[chunk, pl.ds(2, 2)]
        return [
            send(low, low, ahead(1)),
            send(high, high, ahead(-1)),
            send(high, high, ahead(1)),
            send(low, low, ahead(-1)),
        ]

    def spread_third(c, got, place, ahead):
        arrived(got[:1])
        piece = c.all.at[lax.rem(place + 3, 4), pl.ds(0, 2)]
        out = [send(piece, piece, ahead(1))]
        arrived(got[1:2])
        piece = c.all.at[lax.rem(place + 1, 4), pl.ds(2, 2)]
        out.append(send(piece, piece, ahead(-1)))
        return out

    first_h = spread_first(h, x, y, at_y)
    slope_out[...] = slope
    turn = pltpu.make_async_remote_copy(
        src_ref=slope_out, dst_ref=slope_in, send_sem=send_sem.at[COPIES - 1],
        recv_sem=recv_sem.at[COPIES - 1], device_id=turned, device_id_type=MESH,
    )

    @pl.when(x != y)
    def _():
        turn.start()

    @pl.when(x == y)
    def _():
        slope_in[...] = slope_out[...]

    second_g = second_sum(g, direct_g, at_x, x)
    spread_h = spread_second(h, first_h, x, at_x)
    grad_act = summed(g, second_g, x)

    @pl.when(x != y)
    def _():
        turn.wait_recv()

    g.all[y, x] = (grad_act * slope_in[...]).astype(BF16)
    first_g = spread_first(g, y, x, at_x)

    expand = expander()

    def widened(blocks):
        rows = [jnp.concatenate([blocks[2 * up], blocks[2 * up + 1]], axis=1) for up in range(2)]
        return jnp.dot(
            expand, jnp.concatenate(rows, axis=0), preferred_element_type=F32
        ).astype(BF16)

    def mixed_part(rel):
        u = lax.rem(x + rel, 4)
        return jnp.dot(widened(h.all[u]), wout[u], preferred_element_type=F32)

    def grad_in_part(rel):
        u = lax.rem(y + rel, 4)
        return against(widened(g.all[u]), win[u])

    h.acc[...] = mixed_part(0)
    spread_h2 = spread_third(h, spread_h, x, at_x)
    spread_g = spread_second(g, first_g, y, at_y)
    g.acc[...] = grad_in_part(0)
    arrived(spread_h[2:])
    h.acc[...] += mixed_part(1)
    h.acc[...] += mixed_part(3)
    spread_g2 = spread_third(g, spread_g, y, at_y)
    arrived(spread_h2)
    h.acc[...] += mixed_part(2)

    def to_near(c):
        acc = c.acc[...]
        left = acc[:, :half].reshape(16, 8, half)
        right = acc[:, half:].reshape(16, 8, half)
        blocks = jnp.concatenate([left, right], axis=1)
        c.blocks[...] = blocks
        c.sendz[...] = blocks.astype(BF16)
        up = c.sendz.at[pl.ds(lax.rem(z + 3, 4) * 4, 4)]
        down = c.sendz.at[pl.ds(lax.rem(z + 1, 4) * 4, 4)]
        here = lax.rem(z, 4) * 4
        return [
            send(c.sendz.at[pl.ds(here, 2)], c.nearz2.at[pl.ds(0, 2)], at_z(2)),
            send(c.sendz.at[pl.ds(here + 2, 2)], c.nearz2.at[pl.ds(2, 2)], at_z(-2)),
            send(up, c.nearz.at[0], at_z(1)),
            send(down, c.nearz.at[1], at_z(-1)),
        ]

    def to_far(c, got):
        arrived(got)
        total = c.blocks[pl.ds(held, 4)] + c.nearz[0].astype(F32)
        total = total + c.nearz[1].astype(F32) + c.nearz2[...].astype(F32)
        c.sendf[...] = total.astype(BF16)
        out = []
        for n, step in enumerate(FAR):
            there = lax.div(lax.rem(z + step + 16, 16), 4)
            out.append(send(c.sendf.at[there], c.recvf.at[n], at_z(step)))
        return out

    def finish(c, got, n):
        arrived(got)
        total = c.recvf[0].astype(F32) + c.recvf[1].astype(F32)
        total = total + c.recvf[2].astype(F32) + c.recvf[3].astype(F32)
        whole = jnp.concatenate([total[:8], total[8:]], axis=1)
        out_ref[n] = whole[:6].astype(BF16)

    near_h = to_near(h)
    arrived(spread_g[2:])
    g.acc[...] += grad_in_part(1)
    g.acc[...] += grad_in_part(3)
    arrived(spread_g2)
    g.acc[...] += grad_in_part(2)
    near_g = to_near(g)
    far_h = to_far(h, near_h)
    far_g = to_far(g, near_g)
    late = near_g + far_h + far_g
    for copy in started:
        if not any(copy is other for other in late):
            copy.wait_send()

    @pl.when(x != y)
    def _():
        turn.wait_send()

    finish(h, far_h, 0)
    finish(g, far_g, 1)

    for copy in late:
        copy.wait_send()


def shards(tokens, w_in, w_out, grad_out):
    rows, width = tokens.shape
    half = width // 2
    out = jax.ShapeDtypeStruct((2, rows, width), BF16)
    vmem = pl.BlockSpec(memory_space=pltpu.VMEM)
    hbm = pl.BlockSpec(memory_space=pl.ANY)
    both = pl.pallas_call(
        kernel,
        out_shape=out,
        in_specs=[hbm, hbm, hbm, hbm],
        out_specs=vmem,
        scratch_shapes=[
            pltpu.VMEM((4, width, width), BF16),
            pltpu.VMEM((4, width, width), BF16),
            pltpu.VMEM((2,) + tokens.shape, BF16),
            pltpu.VMEM((2, 16, half), BF16),
            pltpu.VMEM((2, 16, 16, half), BF16),
            pltpu.VMEM((48, half), F32),
            pltpu.VMEM((48, half), F32),
        ]
        + chain_scratch(half, width)
        + chain_scratch(half, width)
        + [
            pltpu.SemaphoreType.DMA((6,)),
            pltpu.SemaphoreType.DMA((COPIES,)),
            pltpu.SemaphoreType.DMA((COPIES,)),
        ],
        compiler_params=pltpu.CompilerParams(
            collective_id=0, has_side_effects=True, vmem_limit_bytes=62 * 1024 * 1024
        ),
        cost_estimate=pl.CostEstimate(
            flops=8 * 192 * width * w_in.shape[1], bytes_accessed=4 * w_in.size, transcendentals=0
        ),
    )(tokens, w_in, w_out, grad_out)
    return both[0], both[1]


def solution(mesh):
    placed = (P("col", "row"), P("row", "col"), P("col", "row"), P("col", "row"))
    return jax.shard_map(
        shards,
        mesh=mesh,
        in_specs=placed,
        out_specs=(P("col", "row"), P("col", "row")),
        check_vma=False,
    )
```

profile of v0, /device:TPU:10, one launch (start us, length us, event | category | flops | bytes accessed | tf_op | source)
XLA Modules:
  0.0 71.3 jit_solution(16094466885395292254)
XLA Ops:
  0.6 69.3 %shard_map.59 = bf16[2,6,768]{2,1,0:T(8,128)(2,1)} custom-call(bf16[6,768]{1,0:T(8,128)(2,1)} %tok_ref.1, bf16[768,1536]{1,0:T(8,128)(2,1)} %win_ref.1, bf16[1536,768]{1,0:T(8,128)(2,1)} %wout_ref.1, bf16[6,768]{1,0:T(8,128)(2,1)} %gout_ref.1), custom_call_target="tpu_custom_call" | custom-call | flops 1811939328 | bytes 4718592 | tf_op jit(solution)/shard_map/pallas_call | solution.py:410
  70.0 1.3 %slice_bitcast_fusion = (bf16[6,768]{1,0:T(8,128)(2,1)}, bf16[6,768]{1,0:T(8,128)(2,1)}) fusion(bf16[2,6,768]{2,1,0:T(8,128)(2,1)} %shard_map.59), kind=kLoop, calls=%fused_computation | loop fusion | bytes 36864 | tf_op jit(solution)/shard_map/squeeze | solution.py:438
where the time goes:
time: 71.6 us; the launch traced here: 71.3 us
  Pallas kernels  69.3 us (97%)
  local copies, waits for them, and re-layouts  1.33 us (2%)
    pallas_call x1, Pallas kernels, shards(): pl.pallas_call(kernel, out_shape=out, in_specs=[hbm, hbm, hbm, hbm], out_...  69.3 us

commit v1 on v0

--- a/solution.py
+++ b/solution.py
@@ -42,13 +42,13 @@
         pltpu.VMEM((4, 4) + block, BF16),
         pltpu.VMEM((2, 2) + block, BF16),
         pltpu.VMEM((2, 4) + block, BF16),
-        pltpu.VMEM((4,) + block, F32),
-        pltpu.VMEM((4,) + block, BF16),
+        pltpu.VMEM(block, F32),
+        pltpu.VMEM((3,) + block, BF16),
         pltpu.VMEM((3,) + block, BF16),
         pltpu.VMEM((4, 4) + block, BF16),
         pltpu.VMEM((128, width), F32),
-        pltpu.VMEM((16, 16, half), F32),
-        pltpu.VMEM((16, 16, half), BF16),
+        pltpu.VMEM((4, 16, half), F32),
+        pltpu.VMEM((3, 4, 16, half), BF16),
         pltpu.VMEM((2, 4, 16, half), BF16),
         pltpu.VMEM((4, 16, half), BF16),
         pltpu.VMEM((4, 16, half), BF16),
@@ -61,10 +61,10 @@
 
 
 def kernel(tok_ref, win_ref, wout_ref, gout_ref, out_ref, *scratch):
-    win, wout, raw, own, gathered, slope_out, slope_in = scratch[:7]
-    h = Chain(scratch[7:7 + CHAIN_REFS])
-    g = Chain(scratch[7 + CHAIN_REFS:7 + 2 * CHAIN_REFS])
-    local_sem, send_sem, recv_sem = scratch[7 + 2 * CHAIN_REFS:]
+    win, wout, raw, own, gathered, slope_out, slope_in, picks, expand = scratch[:9]
+    h = Chain(scratch[9:9 + CHAIN_REFS])
+    g = Chain(scratch[9 + CHAIN_REFS:9 + 2 * CHAIN_REFS])
+    local_sem, send_sem, recv_sem = scratch[9 + 2 * CHAIN_REFS:]
     width = tok_ref.shape[1]
     half = width // 2
 
@@ -110,6 +110,18 @@
         whole = jnp.concatenate([raw[n].astype(F32), empty], axis=0)
         folded = jnp.concatenate([whole[:, :half], whole[:, half:]], axis=0)
         own[n] = folded.astype(BF16)
+
+    at = lax.broadcasted_iota(jnp.int32, (96, 256), 0)
+    come = lax.broadcasted_iota(jnp.int32, (96, 256), 1)
+    for side in range(2):
+        within = (come & 15) - 8 * side
+        chosen = (within >= 0) & (within < 6) & (at == 6 * (come >> 4) + within)
+        picks[side] = jnp.where(chosen, 1.0, 0.0).astype(BF16)
+    at = lax.broadcasted_iota(jnp.int32, (128, 96), 0)
+    come = lax.broadcasted_iota(jnp.int32, (128, 96), 1)
+    within = at & 7
+    chosen = (within < 6) & (come == 6 * (at >> 3) + within)
+    expand[...] = jnp.where(chosen, 1.0, 0.0).astype(BF16)
 
     pl.semaphore_wait(barrier, len(partners))
 
@@ -156,21 +168,10 @@
         near_in.append(gather_near(n))
 
     def squeeze(c, n):
-        blocks = gathered[n].astype(F32)
-        left = blocks[:, :8, :].reshape(128, half)
-        right = blocks[:, 8:, :].reshape(128, half)
-        spread = jnp.concatenate([left, right], axis=1).astype(BF16)
-        at = lax.broadcasted_iota(jnp.int32, (96, 128), 0)
-        come = lax.broadcasted_iota(jnp.int32, (96, 128), 1)
-        within = come & 7
-        pick = jnp.where((within < 6) & (at == 6 * (come >> 3) + within), 1.0, 0.0).astype(BF16)
-        c.x[...] = jnp.dot(pick, spread, preferred_element_type=F32).astype(BF16)
-
-    def expander():
-        at = lax.broadcasted_iota(jnp.int32, (128, 96), 0)
-        come = lax.broadcasted_iota(jnp.int32, (128, 96), 1)
-        within = at & 7
-        return jnp.where((within < 6) & (come == 6 * (at >> 3) + within), 1.0, 0.0).astype(BF16)
+        blocks = gathered[n].reshape(256, half)
+        for side in range(2):
+            got = jnp.dot(picks[side], blocks, preferred_element_type=F32)
+            c.x[:, half * side:half * side + half] = got.astype(BF16)
 
     def quarters(value):
         return [
@@ -217,18 +218,20 @@
 
     def second_sum(c, got, ahead, place):
         arrived(got)
-        c.total[...] = c.part[0] + c.near1[0].astype(F32) + c.near1[1].astype(F32)
-        c.send2[...] = c.total[...].astype(BF16)
         out = []
         for n, step in enumerate((2, 1, -1)):
-            there = lax.rem(place + step + 4, 4)
-            out.append(send(c.send2.at[there], c.recv2.at[n], ahead(step)))
-        return out
-
-    def summed(c, got, place):
+            c.send2[n] = first_sum(c, lax.rem(place + step + 4, 4)).astype(BF16)
+            out.append(send(c.send2.at[n], c.recv2.at[n], ahead(step)))
+        c.total[...] = first_sum(c, place)
+        return out
+
+    def first_sum(c, there):
+        return c.part[0, there] + c.near1[0, there].astype(F32) + c.near1[1, there].astype(F32)
+
+    def summed(c, got):
         arrived(got)
         return (
-            c.total[place] + c.recv2[0].astype(F32) + c.recv2[1].astype(F32) + c.recv2[2].astype(F32)
+            c.total[...] + c.recv2[0].astype(F32) + c.recv2[1].astype(F32) + c.recv2[2].astype(F32)
         )
 
     arrived(near_in[0])
@@ -261,7 +264,7 @@
     stay(g, grad_part(0))
     second_h = second_sum(h, direct_h, at_y, y)
     direct_g += passed_on(g, relay_g, at_y)
-    hidden = summed(h, second_h, y)
+    hidden = summed(h, second_h)
     act, slope = gelu_and_slope(hidden)
     h.all[x, y] = act.astype(BF16)
 
@@ -305,7 +308,7 @@
 
     second_g = second_sum(g, direct_g, at_x, x)
     spread_h = spread_second(h, first_h, x, at_x)
-    grad_act = summed(g, second_g, x)
+    grad_act = summed(g, second_g)
 
     @pl.when(x != y)
     def _():
@@ -314,12 +317,10 @@
     g.all[y, x] = (grad_act * slope_in[...]).astype(BF16)
     first_g = spread_first(g, y, x, at_x)
 
-    expand = expander()
-
     def widened(blocks):
         rows = [jnp.concatenate([blocks[2 * up], blocks[2 * up + 1]], axis=1) for up in range(2)]
         return jnp.dot(
-            expand, jnp.concatenate(rows, axis=0), preferred_element_type=F32
+            expand[...], jnp.concatenate(rows, axis=0), preferred_element_type=F32
         ).astype(BF16)
 
     def mixed_part(rel):
@@ -341,26 +342,29 @@
     arrived(spread_h2)
     h.acc[...] += mixed_part(2)
 
+    def folded_class(c, step):
+        first = pl.multiple_of(lax.rem(z + step, 4) * 32, 32)
+        acc = c.acc[pl.ds(first, 32), :]
+        left = acc[:, :half].reshape(4, 8, half)
+        right = acc[:, half:].reshape(4, 8, half)
+        return jnp.concatenate([left, right], axis=1)
+
     def to_near(c):
-        acc = c.acc[...]
-        left = acc[:, :half].reshape(16, 8, half)
-        right = acc[:, half:].reshape(16, 8, half)
-        blocks = jnp.concatenate([left, right], axis=1)
-        c.blocks[...] = blocks
-        c.sendz[...] = blocks.astype(BF16)
-        up = c.sendz.at[pl.ds(lax.rem(z + 3, 4) * 4, 4)]
-        down = c.sendz.at[pl.ds(lax.rem(z + 1, 4) * 4, 4)]
-        here = lax.rem(z, 4) * 4
-        return [
-            send(c.sendz.at[pl.ds(here, 2)], c.nearz2.at[pl.ds(0, 2)], at_z(2)),
-            send(c.sendz.at[pl.ds(here + 2, 2)], c.nearz2.at[pl.ds(2, 2)], at_z(-2)),
-            send(up, c.nearz.at[0], at_z(1)),
-            send(down, c.nearz.at[1], at_z(-1)),
+        c.sendz[0] = folded_class(c, 0).astype(BF16)
+        out = [
+            send(c.sendz.at[0, pl.ds(0, 2)], c.nearz2.at[pl.ds(0, 2)], at_z(2)),
+            send(c.sendz.at[0, pl.ds(2, 2)], c.nearz2.at[pl.ds(2, 2)], at_z(-2)),
         ]
+        c.sendz[1] = folded_class(c, 3).astype(BF16)
+        out.append(send(c.sendz.at[1], c.nearz.at[0], at_z(1)))
+        c.sendz[2] = folded_class(c, 1).astype(BF16)
+        out.append(send(c.sendz.at[2], c.nearz.at[1], at_z(-1)))
+        c.blocks[...] = folded_class(c, 2)
+        return out
 
     def to_far(c, got):
         arrived(got)
-        total = c.blocks[pl.ds(held, 4)] + c.nearz[0].astype(F32)
+        total = c.blocks[...] + c.nearz[0].astype(F32)
         total = total + c.nearz[1].astype(F32) + c.nearz2[...].astype(F32)
         c.sendf[...] = total.astype(BF16)
         out = []
@@ -420,6 +424,8 @@
             pltpu.VMEM((2, 16, 16, half), BF16),
             pltpu.VMEM((48, half), F32),
             pltpu.VMEM((48, half), F32),
+            pltpu.VMEM((2, 96, 256), BF16),
+            pltpu.VMEM((128, 96), BF16),
         ]
         + chain_scratch(half, width)
         + chain_scratch(half, width)

time: 71.6 us -> 71.6 us (level)
  the two profiles are of different devices: /device:TPU:10 before, /device:TPU:8 now
where the time goes in v1:
time: 71.6 us; the launch traced here: 71.3 us
  Pallas kernels  69.3 us (97%)
  local copies, waits for them, and re-layouts  1.33 us (2%)
    pallas_call x1, Pallas kernels, shards(): pl.pallas_call(kernel, out_shape=out, in_specs=[hbm, hbm, hbm, hbm], out_...  69.3 us

profile of v1, /device:TPU:8, one launch (start us, length us, event | category | flops | bytes accessed | tf_op | source)
XLA Modules:
  0.0 71.3 jit_solution(11940775385711093409)
XLA Ops:
  0.6 69.3 %shard_map.59 = bf16[2,6,768]{2,1,0:T(8,128)(2,1)} custom-call(bf16[6,768]{1,0:T(8,128)(2,1)} %tok_ref.1, bf16[768,1536]{1,0:T(8,128)(2,1)} %win_ref.1, bf16[1536,768]{1,0:T(8,128)(2,1)} %wout_ref.1, bf16[6,768]{1,0:T(8,128)(2,1)} %gout_ref.1), custom_call_target="tpu_custom_call" | custom-call | flops 1811939328 | bytes 4718592 | tf_op jit(solution)/shard_map/pallas_call | solution.py:414
  70.0 1.3 %slice_bitcast_fusion = (bf16[6,768]{1,0:T(8,128)(2,1)}, bf16[6,768]{1,0:T(8,128)(2,1)}) fusion(bf16[2,6,768]{2,1,0:T(8,128)(2,1)} %shard_map.59), kind=kLoop, calls=%fused_computation | loop fusion | bytes 36864 | tf_op jit(solution)/shard_map/squeeze | solution.py:444

commit v2 on v1

--- a/solution.py
+++ b/solution.py
@@ -72,11 +72,16 @@
     y, x = lax.div(row, 4), lax.rem(row, 4)
     z, core = lax.div(col, 2), lax.rem(col, 2)
 
-    def at_x(step):
-        return (y * 4 + lax.rem(x + step + 4, 4), col)
-
-    def at_y(step):
-        return (lax.rem(y + step + 4, 4) * 4 + x, col)
+    a = core * x + (1 - core) * y
+    b = core * y + (1 - core) * x
+
+    def at_a(step):
+        there = lax.rem(a + step + 4, 4)
+        return (core * (y * 4 + there) + (1 - core) * (there * 4 + x), col)
+
+    def at_b(step):
+        there = lax.rem(b + step + 4, 4)
+        return (core * (there * 4 + x) + (1 - core) * (y * 4 + there), col)
 
     def at_z(step):
         return (row, lax.rem(z + step + 16, 16) * 2 + core)
@@ -98,8 +103,8 @@
 
     partners = [at_z(step) for step in (6, -6, 2, -2, 1, -1)]
     partners += [other_core, (x * 4 + y, z * 2 + core + same * (1 - 2 * core))]
-    partners += [at_x(step) for step in (2, 1, -1)]
-    partners += [at_y(step) for step in (2, 1, -1)]
+    partners += [at_a(step) for step in (2, 1, -1)]
+    partners += [at_b(step) for step in (2, 1, -1)]
     barrier = pltpu.get_barrier_semaphore()
     for partner in partners:
         pl.semaphore_signal(barrier, inc=1, device_id=partner, device_id_type=MESH)
@@ -241,14 +246,14 @@
     arrived(pushed[:2])
 
     def hidden_part(rel):
-        return quarters(jnp.dot(h.x[...], win[lax.rem(x + rel, 4)], preferred_element_type=F32))
+        return quarters(jnp.dot(h.x[...], win[lax.rem(a + rel, 4)], preferred_element_type=F32))
 
     def grad_part(rel):
-        return quarters(against(g.x[...], wout[lax.rem(y + rel, 4)]))
-
-    relay_h = relays(h, hidden_part(2), at_x)
-    direct_h = direct_up(h, hidden_part(1), at_x)
-    direct_h += direct_down(h, hidden_part(3), at_x)
+        return quarters(against(g.x[...], wout[lax.rem(b + rel, 4)]))
+
+    relay_h = relays(h, hidden_part(2), at_a)
+    direct_h = direct_up(h, hidden_part(1), at_a)
+    direct_h += direct_down(h, hidden_part(3), at_a)
     stay(h, hidden_part(0))
 
     arrived(near_in[1])
@@ -257,16 +262,16 @@
         copy.wait()
     arrived(pushed[2:])
 
-    relay_g = relays(g, grad_part(2), at_y)
-    direct_h += passed_on(h, relay_h, at_x)
-    direct_g = direct_up(g, grad_part(1), at_y)
-    direct_g += direct_down(g, grad_part(3), at_y)
+    relay_g = relays(g, grad_part(2), at_b)
+    direct_h += passed_on(h, relay_h, at_a)
+    direct_g = direct_up(g, grad_part(1), at_b)
+    direct_g += direct_down(g, grad_part(3), at_b)
     stay(g, grad_part(0))
-    second_h = second_sum(h, direct_h, at_y, y)
-    direct_g += passed_on(g, relay_g, at_y)
+    second_h = second_sum(h, direct_h, at_b, b)
+    direct_g += passed_on(g, relay_g, at_b)
     hidden = summed(h, second_h)
     act, slope = gelu_and_slope(hidden)
-    h.all[x, y] = act.astype(BF16)
+    h.all[a, b] = act.astype(BF16)
 
     def spread_first(c, chunk, place, ahead):
         piece = c.all.at[chunk, place]
@@ -291,7 +296,7 @@
         out.append(send(piece, piece, ahead(-1)))
         return out
 
-    first_h = spread_first(h, x, y, at_y)
+    first_h = spread_first(h, a, b, at_b)
     slope_out[...] = slope
     turn = pltpu.make_async_remote_copy(
         src_ref=slope_out, dst_ref=slope_in, send_sem=send_sem.at[COPIES - 1],
@@ -306,16 +311,16 @@
     def _():
         slope_in[...] = slope_out[...]
 
-    second_g = second_sum(g, direct_g, at_x, x)
-    spread_h = spread_second(h, first_h, x, at_x)
+    second_g = second_sum(g, direct_g, at_a, a)
+    spread_h = spread_second(h, first_h, a, at_a)
     grad_act = summed(g, second_g)
 
     @pl.when(x != y)
     def _():
         turn.wait_recv()
 
-    g.all[y, x] = (grad_act * slope_in[...]).astype(BF16)
-    first_g = spread_first(g, y, x, at_x)
+    g.all[b, a] = (grad_act * slope_in[...]).astype(BF16)
+    first_g = spread_first(g, b, a, at_a)
 
     def widened(blocks):
         rows = [jnp.concatenate([blocks[2 * up], blocks[2 * up + 1]], axis=1) for up in range(2)]
@@ -324,21 +329,21 @@
         ).astype(BF16)
 
     def mixed_part(rel):
-        u = lax.rem(x + rel, 4)
+        u = lax.rem(a + rel, 4)
         return jnp.dot(widened(h.all[u]), wout[u], preferred_element_type=F32)
 
     def grad_in_part(rel):
-        u = lax.rem(y + rel, 4)
+        u = lax.rem(b + rel, 4)
         return against(widened(g.all[u]), win[u])
 
     h.acc[...] = mixed_part(0)
-    spread_h2 = spread_third(h, spread_h, x, at_x)
-    spread_g = spread_second(g, first_g, y, at_y)
+    spread_h2 = spread_third(h, spread_h, a, at_a)
+    spread_g = spread_second(g, first_g, b, at_b)
     g.acc[...] = grad_in_part(0)
     arrived(spread_h[2:])
     h.acc[...] += mixed_part(1)
     h.acc[...] += mixed_part(3)
-    spread_g2 = spread_third(g, spread_g, y, at_y)
+    spread_g2 = spread_third(g, spread_g, b, at_b)
     arrived(spread_h2)
     h.acc[...] += mixed_part(2)
 

time: 71.6 us -> 73.9 us (1.032)
  the two profiles are of different devices: /device:TPU:8 before, /device:TPU:2 now
where the time goes in v2:
time: 73.9 us; the launch traced here: 73.6 us
  Pallas kernels  71.6 us (97%)
  local copies, waits for them, and re-layouts  1.33 us (2%)
    pallas_call x1, Pallas kernels, shards(): pl.pallas_call(kernel, out_shape=out, in_specs=[hbm, hbm, hbm, hbm], out_...  71.6 us

profile of v2, /device:TPU:2, one launch (start us, length us, event | category | flops | bytes accessed | tf_op | source)
XLA Modules:
  0.0 73.6 jit_solution(17872361129300610503)
XLA Ops:
  0.6 71.6 %shard_map.59 = bf16[2,6,768]{2,1,0:T(8,128)(2,1)} custom-call(bf16[6,768]{1,0:T(8,128)(2,1)} %tok_ref.1, bf16[768,1536]{1,0:T(8,128)(2,1)} %win_ref.1, bf16[1536,768]{1,0:T(8,128)(2,1)} %wout_ref.1, bf16[6,768]{1,0:T(8,128)(2,1)} %gout_ref.1), custom_call_target="tpu_custom_call" | custom-call | flops 1811939328 | bytes 4718592 | tf_op jit(solution)/shard_map/pallas_call | solution.py:419
  72.3 1.3 %slice_bitcast_fusion = (bf16[6,768]{1,0:T(8,128)(2,1)}, bf16[6,768]{1,0:T(8,128)(2,1)}) fusion(bf16[2,6,768]{2,1,0:T(8,128)(2,1)} %shard_map.59), kind=kLoop, calls=%fused_computation | loop fusion | bytes 36864 | tf_op jit(solution)/shard_map/squeeze | solution.py:449

commit v3 on v0

--- a/solution.py
+++ b/solution.py
@@ -337,7 +337,6 @@
     arrived(spread_h[2:])
     h.acc[...] += mixed_part(1)
     h.acc[...] += mixed_part(3)
-    spread_g2 = spread_third(g, spread_g, y, at_y)
     arrived(spread_h2)
     h.acc[...] += mixed_part(2)
 
@@ -377,6 +376,7 @@
         out_ref[n] = whole[:6].astype(BF16)
 
     near_h = to_near(h)
+    spread_g2 = spread_third(g, spread_g, y, at_y)
     arrived(spread_g[2:])
     g.acc[...] += grad_in_part(1)
     g.acc[...] += grad_in_part(3)

time: 71.6 us -> 71.7 us (level)
  the two profiles are of different devices: /device:TPU:10 before, /device:TPU:8 now
where the time goes in v3:
time: 71.7 us; the launch traced here: 71.4 us
  Pallas kernels  69.4 us (97%)
  local copies, waits for them, and re-layouts  1.33 us (2%)
    pallas_call x1, Pallas kernels, shards(): pl.pallas_call(kernel, out_shape=out, in_specs=[hbm, hbm, hbm, hbm], out_...  69.4 us

profile of v3, /device:TPU:8, one launch (start us, length us, event | category | flops | bytes accessed | tf_op | source)
XLA Modules:
  0.0 71.4 jit_solution(15752373269680020453)
XLA Ops:
  0.6 69.4 %shard_map.59 = bf16[2,6,768]{2,1,0:T(8,128)(2,1)} custom-call(bf16[6,768]{1,0:T(8,128)(2,1)} %tok_ref.1, bf16[768,1536]{1,0:T(8,128)(2,1)} %win_ref.1, bf16[1536,768]{1,0:T(8,128)(2,1)} %wout_ref.1, bf16[6,768]{1,0:T(8,128)(2,1)} %gout_ref.1), custom_call_target="tpu_custom_call" | custom-call | flops 1811939328 | bytes 4718592 | tf_op jit(solution)/shard_map/pallas_call | solution.py:410
  70.1 1.3 %slice_bitcast_fusion = (bf16[6,768]{1,0:T(8,128)(2,1)}, bf16[6,768]{1,0:T(8,128)(2,1)}) fusion(bf16[2,6,768]{2,1,0:T(8,128)(2,1)} %shard_map.59), kind=kLoop, calls=%fused_computation | loop fusion | bytes 36864 | tf_op jit(solution)/shard_map/squeeze | solution.py:438
